TPU v7x, 128 devices: a whole 4x4x4 slice. The times are simulated.
128 devices in a mesh: doc: 4 (over x), clu: 32 (over z, y, core).
Axes of the slice: x: 4, y: 4, z: 4, core: 2. Of those that a mesh axis runs over, the one named last changes fastest.
Arguments:
- embeddings: bfloat16 [16384, 4096], P(('doc', 'clu')), may hold values from -6 to 6
- cluster_ids: int32 [16384, 1], P(('doc', 'clu')), may hold values from 0 to 127; in each aligned block of 128 rows (0 to 127, 128 to 255, ...) at most 3 rows name the same one
Outputs:
- max_similarity: float32 [16384], P(('doc', 'clu'))
Inputs may be any that keep to these rules, and one draw needn't show every extreme that they name: `cluster_ids`: within the 128 rows of one device no cluster id occurs more than 3 times, and in every draw some cluster occurs exactly 3 times among the rows of some device.
All inputs are finite; a program needn't handle non-finite values.
Results may differ from a plain program's by a relative error of at most 0.0016.
Values may be sent and summed in bfloat16 or wider, within the bound.
A program may use at most 64 MiB of HBM per device.

v0:
```python
import jax
import jax.numpy as jnp
from jax import lax
from jax.sharding import PartitionSpec as P


def body(embeddings, cluster_ids):
    features = embeddings.shape[1]
    doc_count = lax.axis_size("doc")
    clu_count = lax.axis_size("clu")
    owners = doc_count * clu_count
    capacity = 3 * embeddings.shape[0] // owners
    values = embeddings.astype(jnp.float32)
    squares = jnp.sum(values * values, axis=1, keepdims=True)
    normed = (values * lax.rsqrt(squares + 1e-06)).astype(jnp.bfloat16)
    cluster = cluster_ids[:, 0]
    one_hot = (cluster[:, None] == jnp.arange(owners, dtype=jnp.int32)[None, :]).astype(jnp.int32)
    earlier = jnp.cumsum(one_hot, axis=0) - one_hot
    position = jnp.sum(earlier * one_hot, axis=1)
    slot_index = cluster * capacity + position
    outgoing = jnp.zeros((owners * capacity, features), jnp.bfloat16).at[slot_index].set(normed)
    occupied = jnp.zeros((owners * capacity,), jnp.bfloat16).at[slot_index].set(1.0)
    incoming, present = (
        lax.all_to_all(
            outgoing.reshape(owners, capacity, features),
            ("doc", "clu"),
            split_axis=0,
            concat_axis=0,
            tiled=True,
        ),
        lax.all_to_all(
            occupied.reshape(owners, capacity),
            ("doc", "clu"),
            split_axis=0,
            concat_axis=0,
            tiled=True,
        ),
    )
    members = incoming.reshape(-1, features)
    present = present.reshape(-1)
    scores = jnp.einsum("id,jd->ij", members, members, preferred_element_type=jnp.float32)
    places = members.shape[0]
    row_iota = lax.broadcasted_iota(jnp.int32, (places, places), 0)
    col_iota = lax.broadcasted_iota(jnp.int32, (places, places), 1)
    allowed = (present[None, :] > 0) & (row_iota != col_iota)
    highest = jnp.max(jnp.where(allowed, scores, jnp.float32(-1.0)), axis=1)
    returned = lax.all_to_all(
        highest.reshape(owners, capacity), ("doc", "clu"), split_axis=0, concat_axis=0, tiled=True
    )
    return returned.reshape(-1)[slot_index]


def solution(mesh):
    return jax.shard_map(
        body,
        mesh=mesh,
        in_specs=(P(("doc", "clu"), None), P(("doc", "clu"), None)),
        out_specs=P(("doc", "clu")),
        check_vma=False,
    )
```

profile of v0, /device:TPU:1, one launch (start us, length us, event | category | flops | bytes accessed | tf_op | source)
XLA Modules:
  0.0 115.8 jit_solution(15195494453606034582)
XLA Ops:
  0.0 0.7 fusion.8
  0.7 0.2 reduce_window_sum.11
  0.9 0.8 select_reduce_fusion
  1.7 0.7 fusion.9
  2.4 1.3 %scatter_custom_fusion = bf16[384]{0:T(512)(128)(2,1)S(1)} fusion(s32[128]{0:T(128)S(1)} %fusion.9, bf16[128]{0:T(256)(128)(2,1)S(1)} %broadcast.27, bf16[]{:T(256)} %constant.9.clone.1), kind=kCustom, calls=%fused_computation.23 | custom fusion | bytes 770 | tf_op jit(solution)/shard_map/scatter | solution.py:22
  3.8 0.9 all_to_all.20
  4.7 11.5 %all-to-all-start = ((bf16[128,1,3]{2,1,0:T(2,128)(2,1)}), bf16[128,1,3]{2,1,0:T(2,128)(2,1)S(1)}, u32[]{:S(2)}, u32[]{:S(2)}) async-start(bf16[128,1,3]{2,1,0:T(2,128)(2,1)} %all_to_all.20), calls=%async_computation | async-start | bytes 131072 | tf_op jit(solution)/shard_map/all_to_all | solution.py:31
  16.2 1.5 %fusion = f32[128]{0:T(128)S(1)} fusion(bf16[128,4096]{1,0:T(8,128)(2,1)} %param.2), kind=kLoop, calls=%fused_computation.5 | loop fusion | flops 1572736 | bytes 1049088 | tf_op jit(solution)/shard_map/reduce_sum | solution.py:14
  17.7 3.9 %scatter_custom_fusion.1 = bf16[384,4096]{1,0:T(8,128)(2,1)S(1)} fusion(s32[128]{0:T(128)S(1)} %fusion.9, bf16[]{:T(256)} %constant.9.clone.1, bf16[128,4096]{1,0:T(8,128)(2,1)} %param.2, f32[128]{0:T(128)S(1)} %add_rsqrt_fusion), kind=kCustom, calls=%fused_computation.7 | custom fusion | flops 1572864 | bytes 4194818 | tf_op jit(solution)/shard_map/scatter | solution.py:21
  21.6 4.4 %reshape.35 = bf16[128,3,4096]{2,1,0:T(4,128)(2,1)} reshape(bf16[384,4096]{1,0:T(8,128)(2,1)S(1)} %scatter_custom_fusion.1) | data formatting | bytes 6291456 | tf_op jit(solution)/shard_map/reshape | solution.py:25
  26.0 0.0 all-to-all-done
  26.0 10.2 %all-to-all-start.1 = ((bf16[128,3,4096]{2,1,0:T(4,128)(2,1)}), bf16[128,3,4096]{2,1,0:T(4,128)(2,1)}, u32[]{:S(2)}, u32[]{:S(2)}) async-start(bf16[128,3,4096]{2,1,0:T(4,128)(2,1)} %reshape.35), calls=%async_computation.1 | async-start | bytes 8388608 | tf_op jit(solution)/shard_map/all_to_all | solution.py:24
  36.3 0.2 compare_reduce_fusion
  36.5 0.2 gt.13
  36.7 52.1 %all-to-all-done.1 = bf16[128,3,4096]{2,1,0:T(4,128)(2,1)} async-done(((bf16[128,3,4096]{2,1,0:T(4,128)(2,1)}), bf16[128,3,4096]{2,1,0:T(4,128)(2,1)}, u32[]{:S(2)}, u32[]{:S(2)}) %all-to-all-start.1) | async-done | bytes 3145760 | tf_op jit(solution)/shard_map/all_to_all | solution.py:24
  88.8 6.0 %reshape.36 = bf16[384,4096]{1,0:T(8,128)(2,1)S(1)} reshape(bf16[128,3,4096]{2,1,0:T(4,128)(2,1)} %all-to-all-done.1) | data formatting | bytes 6291456 | tf_op jit(solution)/shard_map/reshape | solution.py:39
  94.8 1.8 %fusion.4 = f32[384]{0:T(512)S(1)} fusion(bf16[384,4096]{1,0:T(8,128)(2,1)S(1)} %reshape.36, pred[384]{0:T(512)(128)(4,1)S(1)} %gt.13), kind=kOutput, calls=%fused_computation.10 | convolution fusion | flops 1208548992 | bytes 3147648 | tf_op jit(solution)/shard_map/id,jd->ij/dot_general | solution.py:41
  96.6 0.8 all_to_all.18
  97.4 5.6 %all-to-all-start.2 = ((f32[128,1,3]{2,1,0:T(1,128)}), f32[128,1,3]{2,1,0:T(1,128)S(1)}, u32[]{:S(2)}, u32[]{:S(2)}) async-start(f32[128,1,3]{2,1,0:T(1,128)} %bitcast.3), calls=%async_computation.2 | async-start | bytes 131072 | tf_op jit(solution)/shard_map/all_to_all | solution.py:47
  103.1 9.5 %all-to-all-done.2 = f32[128,1,3]{2,1,0:T(1,128)S(1)} async-done(((f32[128,1,3]{2,1,0:T(1,128)}), f32[128,1,3]{2,1,0:T(1,128)S(1)}, u32[]{:S(2)}, u32[]{:S(2)}) %all-to-all-start.2) | async-done | bytes 1568 | tf_op jit(solution)/shard_map/all_to_all | solution.py:47
  112.5 0.5 broadcast.39
  113.1 0.8 reduce.5
  113.9 0.2 reshape.37
  114.1 1.8 %gather_fusion = f32[128]{0:T(128)} fusion(f32[384]{0:T(512)S(1)} %reshape.37, s32[1024]{0:T(1024)S(1)} %pad_clamp_fusion), kind=kCustom, calls=%fused_computation | custom fusion | bytes 1536 | tf_op jit(solution)/shard_map/gather | solution.py:50
  (3 shorter events, 0.0 us)
Async XLA Ops:
  4.7 21.4 %all-to-all-start = ((bf16[128,1,3]{2,1,0:T(2,128)(2,1)}), bf16[128,1,3]{2,1,0:T(2,128)(2,1)S(1)}, u32[]{:S(2)}, u32[]{:S(2)}) async-start(bf16[128,1,3]{2,1,0:T(2,128)(2,1)} %all_to_all.20), calls=%async_computation | async-start | bytes 131072 | tf_op jit(solution)/shard_map/all_to_all | solution.py:31
  26.0 62.8 %all-to-all-start.1 = ((bf16[128,3,4096]{2,1,0:T(4,128)(2,1)}), bf16[128,3,4096]{2,1,0:T(4,128)(2,1)}, u32[]{:S(2)}, u32[]{:S(2)}) async-start(bf16[128,3,4096]{2,1,0:T(4,128)(2,1)} %reshape.35), calls=%async_computation.1 | async-start | bytes 8388608 | tf_op jit(solution)/shard_map/all_to_all | solution.py:24
  97.4 15.1 %all-to-all-start.2 = ((f32[128,1,3]{2,1,0:T(1,128)}), f32[128,1,3]{2,1,0:T(1,128)S(1)}, u32[]{:S(2)}, u32[]{:S(2)}) async-start(f32[128,1,3]{2,1,0:T(1,128)} %bitcast.3), calls=%async_computation.2 | async-start | bytes 131072 | tf_op jit(solution)/shard_map/all_to_all | solution.py:47
where the time goes:
time: 116 us
  waiting for transfers between devices  61.6 us (53%)
  starting transfers between devices  27.3 us (24%)
  local copies, waits for them, and re-layouts  16.2 us (14%)
  other arithmetic  8.88 us (8%)
  matrix products  1.82 us (2%)
    all_to_all x1, waiting for transfers between devices, body(): lax.all_to_all(outgoing.reshape(owners, capacity, features), ('doc', 'clu...  52.1 us
    all_to_all x1, starting transfers between devices, body(): lax.all_to_all(occupied.reshape(owners, capacity), ('doc', 'clu'), split_...  11.5 us
    all_to_all x1, starting transfers between devices, body(): lax.all_to_all(outgoing.reshape(owners, capacity, features), ('doc', 'clu...  10.2 us
    all_to_all x1, waiting for transfers between devices, body(): lax.all_to_all(highest.reshape(owners, capacity), ('doc', 'clu'), split_a...  9.49 us
    reshape x1, local copies, waits for them, and re-layouts, body(): members = incoming.reshape(-1, features)  5.96 us
    all_to_all x1, starting transfers between devices, body(): lax.all_to_all(highest.reshape(owners, capacity), ('doc', 'clu'), split_a...  5.59 us
    reshape x1, local copies, waits for them, and re-layouts, body(): outgoing.reshape(owners, capacity, features)  4.44 us
    scatter x1, other arithmetic, body(): jnp.zeros((owners * capacity, features), jnp.bfloat16).at[slot_index]  3.91 us
  transfers between devices with their start and end apart: 3, of which 2 were waited for; matrix products, arithmetic and copies ran while one was open for 9% of the time, Pallas kernels for 0%

commit v1 on v0

v1 whole, which is shorter than its diff:
```python
import functools

import jax
import jax.numpy as jnp
from jax import lax
from jax.experimental import pallas as pl
from jax.experimental.pallas import tpu as pltpu
from jax.sharding import PartitionSpec as P

MESH = pl.DeviceIdType.MESH
DEVICES = 128
ROWS = 128
CAP = 3
D = 4096
Q = 16
W = D // Q
GROUP = 16
GROUPS = DEVICES // GROUP
EMPTY = 8.0
EMPTY_SQUARES = 50.0 * D
STRIDE = 53
UNSTRIDE = pow(STRIDE, -1, DEVICES)


def position():
    doc, clu = lax.axis_index("doc"), lax.axis_index("clu")
    return doc, clu // 8, (clu // 2) % 4, clu % 2


def offsets(n):
    place = (STRIDE * (n + 1) + DEVICES - 1) % DEVICES
    core = 1 - place % 2
    x = 3 - (place // 2) % 4
    y = 3 - (place // 8) % 4
    z = 3 - place // 32
    return x, z, y, core


def device(x, z, y, core):
    return x % 4, (z % 4) * 8 + (y % 4) * 2 + core % 2


def target(me, n):
    return device(*(a + b for a, b in zip(me, offsets(n))))


def origin(me, n):
    return device(*(a + 4 - b for a, b in zip(me, offsets(n))))


def slot_of(cluster, me):
    x, z, y, core = me
    dx = (cluster // 32 + 4 - x) % 4
    dz = ((cluster // 8) % 4 + 4 - z) % 4
    dy = ((cluster // 2) % 4 + 4 - y) % 4
    dc = (cluster % 2 + 2 - core) % 2
    place = (((3 - dz) * 4 + (3 - dy)) * 4 + (3 - dx)) * 2 + (1 - dc)
    return (UNSTRIDE * (place + 1) + DEVICES - 1) % DEVICES


def kernel(
    ids_ref, emb_ref, out_ref,
    blocks, outgoing, incoming, members, gram, index_v, index_s, highest, returned,
    index_sem, send_sem, recv_sem, back_send_sem, back_recv_sem,
):
    me = position()
    barrier = pltpu.get_barrier_semaphore()

    @pl.loop(0, DEVICES - 1)
    def _(n):
        pl.semaphore_signal(barrier, inc=1, device_id=target(me, n), device_id_type=MESH)

    rows = lax.broadcasted_iota(jnp.int32, (ROWS, DEVICES), 0)
    lanes = lax.broadcasted_iota(jnp.int32, (ROWS, DEVICES), 1)
    named = slot_of(ids_ref[...], me) == lanes
    earlier = jnp.dot(
        (lanes < rows).astype(jnp.bfloat16), named.astype(jnp.bfloat16), preferred_element_type=jnp.float32
    )
    place = jnp.sum(jnp.where(named, earlier, 0.0), axis=1, keepdims=True)
    for p in range(CAP):
        here = named & (earlier == p)
        row = ROWS + jnp.sum(jnp.where(here, rows - ROWS, 0), axis=0, keepdims=True)
        index_v[p : p + 1, :] = jnp.clip(row, 0, ROWS)
    to_scalars = pltpu.make_async_copy(index_v, index_s, index_sem)
    to_scalars.start()

    a = lax.broadcasted_iota(jnp.int32, (GROUP * Q, GROUP * Q), 0)
    b = lax.broadcasted_iota(jnp.int32, (GROUP * Q, GROUP * Q), 1)
    swap = ((a // Q == b % GROUP) & (a % Q == b // GROUP)).astype(jnp.bfloat16)

    for g in range(ROWS // GROUP):
        group = pl.ds(g * GROUP, GROUP)
        parts = jnp.concatenate([emb_ref[group, q * W : (q + 1) * W] for q in range(Q)], axis=0)
        swapped = jnp.dot(swap, parts, preferred_element_type=jnp.float32).astype(jnp.bfloat16)
        blocks[group] = swapped.reshape(GROUP, Q, W)
    blocks[ROWS] = jnp.full((Q, W), EMPTY, jnp.bfloat16)

    to_scalars.wait()
    pl.semaphore_wait(barrier, DEVICES - 1)

    @pl.loop(0, DEVICES - 1)
    def _(n):
        for p in range(CAP):
            outgoing[n, p] = blocks[index_s[p, n]]
        pltpu.make_async_remote_copy(
            src_ref=outgoing.at[n],
            dst_ref=incoming.at[n],
            send_sem=send_sem,
            recv_sem=recv_sem.at[n // GROUP],
            device_id=target(me, n),
            device_id_type=MESH,
        ).start()

    for p in range(CAP):
        incoming[DEVICES - 1, p] = blocks[index_s[p, DEVICES - 1]]

    @pl.loop(0, GROUPS)
    def _(g):
        @pl.when(g < GROUPS - 1)
        def _():
            arrived = incoming.at[pl.ds(g * GROUP, GROUP)]
            pltpu.make_async_copy(arrived, arrived, recv_sem.at[g]).wait()

        @pl.when(g == GROUPS - 1)
        def _():
            arrived = incoming.at[pl.ds(DEVICES - GROUP, GROUP - 1)]
            pltpu.make_async_copy(arrived, arrived, recv_sem.at[g]).wait()

        for p in range(CAP):
            parts = incoming[pl.ds(g * GROUP, GROUP), p].reshape(GROUP * Q, W)
            swapped = jnp.dot(swap, parts, preferred_element_type=jnp.float32).astype(jnp.bfloat16)
            where = pl.ds(pl.multiple_of(p * DEVICES + g * GROUP, GROUP), GROUP)
            for q in range(Q):
                members[where, q * W : (q + 1) * W] = swapped[q * GROUP : (q + 1) * GROUP]

    gram[...] = jnp.zeros_like(gram)

    @pl.loop(0, 8)
    def _(k):
        part = members[:, pl.ds(pl.multiple_of(k * 512, 512), 512)]
        gram[...] += lax.dot_general(part, part, (((1,), (1,)), ((), ())), preferred_element_type=jnp.float32)

    places = CAP * DEVICES
    i = lax.broadcasted_iota(jnp.int32, (places, places), 0)
    j = lax.broadcasted_iota(jnp.int32, (places, places), 1)
    products = gram[...]
    own = jnp.where(i == j, products, 0.0)
    squares_i, squares_j = jnp.sum(own, axis=1, keepdims=True), jnp.sum(own, axis=0, keepdims=True)
    scores = products * lax.rsqrt(squares_i + 1e-06) * lax.rsqrt(squares_j + 1e-06)
    allowed = (squares_j < EMPTY_SQUARES) & (i != j)
    best = jnp.max(jnp.where(allowed, scores, -1.0), axis=1, keepdims=True)
    by_place = jnp.where(
        lanes == 0, best[:DEVICES], jnp.where(lanes == 1, best[DEVICES : 2 * DEVICES], best[2 * DEVICES :])
    )
    highest[...] = by_place.reshape(DEVICES, 1, 128)
    returned[DEVICES - 1] = by_place[DEVICES - 1 :]

    @pl.loop(0, DEVICES - 1)
    def _(n):
        pltpu.make_async_remote_copy(
            src_ref=highest.at[n],
            dst_ref=returned.at[n],
            send_sem=back_send_sem,
            recv_sem=back_recv_sem,
            device_id=origin(me, n),
            device_id_type=MESH,
        ).start()

    sent = outgoing.at[pl.ds(0, DEVICES - 1)]
    pltpu.make_async_copy(sent, sent, send_sem).wait()
    back = returned.at[pl.ds(0, DEVICES - 1)]
    pltpu.make_async_copy(back, back, back_recv_sem).wait()
    pltpu.make_async_copy(back, back, back_send_sem).wait()

    mine = jnp.dot(
        named.astype(jnp.float32),
        returned[...].reshape(DEVICES, 128),
        precision=lax.Precision.HIGHEST,
        preferred_element_type=jnp.float32,
    )
    column = jnp.sum(jnp.where(lanes == place.astype(jnp.int32), mine, 0.0), axis=1, keepdims=True)
    out_ref[...] = jnp.sum(jnp.where(rows == lanes, column, 0.0), axis=0, keepdims=True)


def body(embeddings, cluster_ids):
    vmem = pl.BlockSpec(memory_space=pltpu.VMEM)
    out = pl.pallas_call(
        kernel,
        out_shape=jax.ShapeDtypeStruct((1, ROWS), jnp.float32),
        in_specs=[vmem, vmem],
        out_specs=vmem,
        scratch_shapes=[
            pltpu.VMEM((ROWS + 1, Q, W), jnp.bfloat16),
            pltpu.VMEM((DEVICES, CAP, Q, W), jnp.bfloat16),
            pltpu.VMEM((DEVICES, CAP, Q, W), jnp.bfloat16),
            pltpu.VMEM((CAP * DEVICES, D), jnp.bfloat16),
            pltpu.VMEM((CAP * DEVICES, CAP * DEVICES), jnp.float32),
            pltpu.VMEM((8, 128), jnp.int32),
            pltpu.SMEM((8, 128), jnp.int32),
            pltpu.VMEM((DEVICES, 1, 128), jnp.float32),
            pltpu.VMEM((DEVICES, 1, 128), jnp.float32),
            pltpu.SemaphoreType.DMA,
            pltpu.SemaphoreType.DMA,
            pltpu.SemaphoreType.DMA((GROUPS,)),
            pltpu.SemaphoreType.DMA,
            pltpu.SemaphoreType.DMA,
        ],
        compiler_params=pltpu.CompilerParams(
            collective_id=0, has_side_effects=True, vmem_limit_bytes=40 * 1024 * 1024
        ),
    )(cluster_ids, embeddings)
    return out.reshape(ROWS)


def solution(mesh):
    return jax.shard_map(
        body,
        mesh=mesh,
        in_specs=(P(("doc", "clu"), None), P(("doc", "clu"), None)),
        out_specs=P(("doc", "clu")),
        check_vma=False,
    )
```

time: 116 us -> 71.3 us (0.61)
  Pallas kernels: 0 us -> 68.6 us
  waiting for transfers between devices: 61.6 us -> 0 us
  starting transfers between devices: 27.3 us -> 0 us
  local copies, waits for them, and re-layouts: 16.2 us -> 2.49 us
  other arithmetic: 8.88 us -> 0 us
  matrix products: 1.82 us -> 0 us
    pallas_call x0 -> x1, Pallas kernels: none -> 68.6 us  [body(): pl.pallas_call(kernel, out_shape=jax.ShapeDtypeStruct((1, ROWS), jnp.floa...]
    all_to_all x3 -> x0, waiting for transfers between devices: 61.6 us -> none  [the longest x1 52.1 us: body(): lax.all_to_all(outgoing.reshape(owners, capacity, features), ('doc', 'clu...]
    all_to_all x3 -> x0, starting transfers between devices: 27.3 us -> none  [the longest x1 11.5 us: body(): lax.all_to_all(occupied.reshape(owners, capacity), ('doc', 'clu'), split_...]
    reshape x3 -> x0, local copies, waits for them, and re-layouts: 10.6 us -> none  [the longest x1 5.96 us: body(): members = incoming.reshape(-1, features)]
    scatter x1 -> x0, other arithmetic: 3.91 us -> none  [body(): jnp.zeros((owners * capacity, features), jnp.bfloat16).at[slot_index]]
    unnamed x0 -> x4, local copies, waits for them, and re-layouts: none -> 2.49 us
    reduce_sum x2 -> x0, other arithmetic: 2.34 us -> none  [the longest x1 1.52 us: body(): squares = jnp.sum(values * values, axis=1, keepdims=True)]
    all_to_all x3 -> x0, local copies, waits for them, and re-layouts: 2.23 us -> none  [the longest x2 1.34 us: body(): lax.all_to_all(highest.reshape(owners, capacity), ('doc', 'clu'), split_a...]
  transfers between devices with their start and end apart: 3 -> 0, of which waited for: 2 -> 0; matrix products, arithmetic and copies ran while one was open for 9% -> 0% of each run, Pallas kernels for 0% -> 0%
where the time goes in v1:
time: 71.3 us; the launch traced here: 71.2 us
  Pallas kernels  68.6 us (96%)
  local copies, waits for them, and re-layouts  2.49 us (3%)
    pallas_call x1, Pallas kernels, body(): pl.pallas_call(kernel, out_shape=jax.ShapeDtypeStruct((1, ROWS), jnp.floa...  68.6 us
    unnamed x4, local copies, waits for them, and re-layouts  2.49 us

profile of v1, /device:TPU:1, one launch (start us, length us, event | category | flops | bytes accessed | tf_op | source)
XLA Modules:
  0.0 71.2 jit_solution(17493704981488291352)
XLA Ops:
  0.0 0.8 %copy.3.ids_ref = s32[128,1]{1,0:T(8,128)S(1)} copy(s32[128,1]{0,1:T(1,128)} %param.3) | data formatting | bytes 1024 | tf_op args[1]
  0.8 0.0 copy-start
  0.8 1.2 %copy-done = bf16[128,4096]{1,0:T(8,128)(2,1)S(1)} copy-done((bf16[128,4096]{1,0:T(8,128)(2,1)S(1)}, bf16[128,4096]{1,0:T(8,128)(2,1)}, u32[]{:S(2)}) %copy-start) | copy-done | bytes 1048600
  2.0 68.6 %shard_map.28 = f32[1,128]{1,0:T(1,128)S(1)} custom-call(s32[128,1]{1,0:T(8,128)S(1)} %copy.3.ids_ref, bf16[128,4096]{1,0:T(8,128)(2,1)S(1)} %copy-done), custom_call_target="tpu_custom_call" | custom-call | tf_op jit(solution)/shard_map/pallas_call | solution.py:187
  70.6 0.5 copy.5
Async XLA Ops:
  0.8 1.2 %copy-start = (bf16[128,4096]{1,0:T(8,128)(2,1)S(1)}, bf16[128,4096]{1,0:T(8,128)(2,1)}, u32[]{:S(2)}) copy-start(bf16[128,4096]{1,0:T(8,128)(2,1)} %emb_ref.1) | copy-start | bytes 3145732

commit v2 on v1

v2 whole, which is shorter than its diff:
```python
import random

import jax
import jax.numpy as jnp
from jax import lax
from jax.experimental import pallas as pl
from jax.experimental.pallas import tpu as pltpu
from jax.sharding import PartitionSpec as P

MESH = pl.DeviceIdType.MESH
DEVICES = 128
ROWS = 128
CAP = 3
D = 4096
Q = 16
W = D // Q
GROUP = 16
GROUPS = DEVICES // GROUP
EMPTY = 1.0
EMPTY_SCORE = 2.0


def order():
    every = [(x, z, y, c) for x in range(4) for z in range(4) for y in range(4) for c in range(2)]
    random.Random(0).shuffle(every)
    return sorted(every, key=lambda o: (-sum(min(k, 4 - k) for k in o[:3]), -o[3]))


ORDER = order()


def code(o):
    return ((o[0] * 4 + o[1]) * 4 + o[2]) * 2 + o[3]


def position():
    doc, clu = lax.axis_index("doc"), lax.axis_index("clu")
    return doc, clu // 8, (clu // 2) % 4, clu % 2


class Around:
    def __init__(self, me):
        x, z, y, c = me
        self.x = [(x + k) % 4 for k in range(4)]
        self.z = [((z + k) % 4) * 8 for k in range(4)]
        self.y = [((y + k) % 4) * 2 for k in range(4)]
        self.c = [c, 1 - c]

    def to(self, o):
        return self.x[o[0]], self.z[o[1]] + self.y[o[2]] + self.c[o[3]]

    def back(self, o):
        return self.to((-o[0] % 4, -o[1] % 4, -o[2] % 4, o[3]))


def code_of(cluster, me):
    x, z, y, c = me
    dx = ((cluster >> 5) + (4 - x)) & 3
    dz = ((cluster >> 3) + (4 - z)) & 3
    dy = ((cluster >> 1) + (4 - y)) & 3
    dc = (cluster + c) & 1
    return ((dx * 4 + dz) * 4 + dy) * 2 + dc


def kernel(
    ids_hbm, emb_hbm, out_ref,
    ids_ref, emb_ref, blocks, outgoing, incoming, members, index_v, index_s, highest, returned,
    ids_sem, emb_sem, index_sem, send_sem, recv_sem, back_send_sem, back_recv_sem,
):
    me = position()
    around = Around(me)
    barrier = pltpu.get_barrier_semaphore()

    ids_in = pltpu.make_async_copy(ids_hbm, ids_ref, ids_sem)
    ids_in.start()
    rows_in = []
    for g in range(ROWS // GROUP):
        group = pl.ds(g * GROUP, GROUP)
        rows_in.append(pltpu.make_async_copy(emb_hbm.at[group], emb_ref.at[group], emb_sem.at[g]))
        rows_in[g].start()

    for o in ORDER[:-1]:
        pl.semaphore_signal(barrier, inc=1, device_id=around.back(o), device_id_type=MESH)

    rows = lax.broadcasted_iota(jnp.int32, (ROWS, DEVICES), 0)
    lanes = lax.broadcasted_iota(jnp.int32, (ROWS, DEVICES), 1)
    ids_in.wait()
    codes = code_of(ids_ref[...], me)
    named = jnp.transpose(jnp.broadcast_to(codes, (DEVICES, ROWS))) == lanes
    earlier = jnp.dot(
        (lanes < rows).astype(jnp.bfloat16), named.astype(jnp.bfloat16), preferred_element_type=jnp.float32
    )
    place = jnp.sum(jnp.where(named, earlier, 0.0), axis=1, keepdims=True)
    for p in range(CAP):
        here = named & (earlier == p)
        row = ROWS + jnp.sum(jnp.where(here, rows - ROWS, 0), axis=0, keepdims=True)
        index_v[p : p + 1, :] = jnp.clip(row, 0, ROWS)
    to_scalars = pltpu.make_async_copy(index_v, index_s, index_sem)
    to_scalars.start()

    a = lax.broadcasted_iota(jnp.int32, (GROUP * Q, GROUP * Q), 0)
    b = lax.broadcasted_iota(jnp.int32, (GROUP * Q, GROUP * Q), 1)
    swap = ((a // Q == b % GROUP) & (a % Q == b // GROUP)).astype(jnp.bfloat16)

    blocks[ROWS] = jnp.full((Q, W), EMPTY, jnp.bfloat16)
    for g in range(ROWS // GROUP):
        rows_in[g].wait()
        values = emb_ref[pl.ds(g * GROUP, GROUP)].astype(jnp.float32)
        squares = jnp.sum(values * values, axis=1, keepdims=True)
        normed = (values * lax.rsqrt(squares + 1e-06)).astype(jnp.bfloat16)
        parts = jnp.concatenate([normed[:, q * W : (q + 1) * W] for q in range(Q)], axis=0)
        swapped = jnp.dot(swap, parts, preferred_element_type=jnp.float32).astype(jnp.bfloat16)
        blocks[pl.ds(g * GROUP, GROUP)] = swapped.reshape(GROUP, Q, W)

    to_scalars.wait()
    pl.semaphore_wait(barrier, DEVICES - 1)

    for n, o in enumerate(ORDER[:-1]):
        for p in range(CAP):
            outgoing[n, p] = blocks[index_s[p, code(o)]]
        pltpu.make_async_remote_copy(
            src_ref=outgoing.at[n],
            dst_ref=incoming.at[n],
            send_sem=send_sem,
            recv_sem=recv_sem.at[n // GROUP],
            device_id=around.to(o),
            device_id_type=MESH,
        ).start()

    for p in range(CAP):
        incoming[DEVICES - 1, p] = blocks[index_s[p, 0]]

    def arrive(g, count):
        arrived = incoming.at[pl.ds(g * GROUP, count)]
        pltpu.make_async_copy(arrived, arrived, recv_sem.at[g]).wait()
        for p in range(CAP):
            parts = incoming[pl.ds(g * GROUP, GROUP), p].reshape(GROUP * Q, W)
            swapped = jnp.dot(swap, parts, preferred_element_type=jnp.float32).astype(jnp.bfloat16)
            where = pl.ds(pl.multiple_of(p * DEVICES + g * GROUP, GROUP), GROUP)
            for q in range(Q):
                members[where, q * W : (q + 1) * W] = swapped[q * GROUP : (q + 1) * GROUP]

    @pl.loop(0, GROUPS - 1)
    def _(g):
        arrive(g, GROUP)

    arrive(GROUPS - 1, GROUP - 1)

    places = CAP * DEVICES
    scores = lax.dot_general(
        members[...], members[...], (((1,), (1,)), ((), ())), preferred_element_type=jnp.float32
    )
    i = lax.broadcasted_iota(jnp.int32, (places, places), 0)
    j = lax.broadcasted_iota(jnp.int32, (places, places), 1)
    own = jnp.sum(jnp.where(i == j, scores, 0.0), axis=0, keepdims=True)
    allowed = (own < EMPTY_SCORE) & (i != j)
    best = jnp.max(jnp.where(allowed, scores, -1.0), axis=1, keepdims=True)
    by_place = jnp.where(
        lanes == 0, best[:DEVICES], jnp.where(lanes == 1, best[DEVICES : 2 * DEVICES], best[2 * DEVICES :])
    )
    highest[...] = by_place.reshape(DEVICES, 1, 128)
    returned[0] = by_place[DEVICES - 1 :]

    for n, o in enumerate(ORDER[:-1]):
        pltpu.make_async_remote_copy(
            src_ref=highest.at[n],
            dst_ref=returned.at[code(o)],
            send_sem=back_send_sem,
            recv_sem=back_recv_sem,
            device_id=around.back(o),
            device_id_type=MESH,
        ).start()

    back = returned.at[pl.ds(1, DEVICES - 1)]
    pltpu.make_async_copy(back, back, back_recv_sem).wait()

    mine = jnp.dot(
        named.astype(jnp.float32),
        returned[...].reshape(DEVICES, 128),
        precision=lax.Precision.HIGHEST,
        preferred_element_type=jnp.float32,
    )
    column = jnp.sum(jnp.where(lanes == place.astype(jnp.int32), mine, 0.0), axis=1, keepdims=True)
    out_ref[...] = jnp.sum(jnp.where(rows == lanes, column, 0.0), axis=0, keepdims=True)

    sent = outgoing.at[pl.ds(0, DEVICES - 1)]
    pltpu.make_async_copy(sent, sent, send_sem).wait()
    pltpu.make_async_copy(back, back, back_send_sem).wait()


def body(embeddings, cluster_ids):
    hbm = pl.BlockSpec(memory_space=pltpu.HBM)
    out = pl.pallas_call(
        kernel,
        out_shape=jax.ShapeDtypeStruct((1, ROWS), jnp.float32),
        in_specs=[hbm, hbm],
        out_specs=pl.BlockSpec(memory_space=pltpu.VMEM),
        scratch_shapes=[
            pltpu.VMEM((1, ROWS), jnp.int32),
            pltpu.VMEM((ROWS, D), jnp.bfloat16),
            pltpu.VMEM((ROWS + 1, Q, W), jnp.bfloat16),
            pltpu.VMEM((DEVICES, CAP, Q, W), jnp.bfloat16),
            pltpu.VMEM((DEVICES, CAP, Q, W), jnp.bfloat16),
            pltpu.VMEM((CAP * DEVICES, D), jnp.bfloat16),
            pltpu.VMEM((8, 128), jnp.int32),
            pltpu.SMEM((8, 128), jnp.int32),
            pltpu.VMEM((DEVICES, 1, 128), jnp.float32),
            pltpu.VMEM((DEVICES, 1, 128), jnp.float32),
            pltpu.SemaphoreType.DMA,
            pltpu.SemaphoreType.DMA((ROWS // GROUP,)),
            pltpu.SemaphoreType.DMA,
            pltpu.SemaphoreType.DMA,
            pltpu.SemaphoreType.DMA((GROUPS,)),
            pltpu.SemaphoreType.DMA,
            pltpu.SemaphoreType.DMA,
        ],
        compiler_params=pltpu.CompilerParams(
            collective_id=0, has_side_effects=True, vmem_limit_bytes=62 * 1024 * 1024
        ),
    )(cluster_ids.reshape(1, ROWS), embeddings)
    return out.reshape(ROWS)


def solution(mesh):
    return jax.shard_map(
        body,
        mesh=mesh,
        in_specs=(P(("doc", "clu"), None), P(("doc", "clu"), None)),
        out_specs=P(("doc", "clu")),
        check_vma=False,
    )
```

time: 71.3 us -> 57.8 us (0.81)
  Pallas kernels: 68.6 us -> 56.6 us
  local copies, waits for them, and re-layouts: 2.49 us -> 1.1 us
    pallas_call x1, Pallas kernels: 68.6 us -> 56.6 us  [body(): pl.pallas_call(kernel, out_shape=jax.ShapeDtypeStruct((1, ROWS), jnp.floa...]
    unnamed x4 -> x3, local copies, waits for them, and re-layouts: 2.49 us -> 1.1 us
where the time goes in v2:
time: 57.8 us; the launch traced here: 57.7 us
  Pallas kernels  56.6 us (98%)
  local copies, waits for them, and re-layouts  1.1 us (2%)
    pallas_call x1, Pallas kernels, body(): pl.pallas_call(kernel, out_shape=jax.ShapeDtypeStruct((1, ROWS), jnp.floa...  56.6 us

profile of v2, /device:TPU:1, one launch (start us, length us, event | category | flops | bytes accessed | tf_op | source)
XLA Modules:
  0.0 57.7 jit_solution(10376713937762765172)
XLA Ops:
  0.0 56.6 %shard_map.28 = f32[1,128]{1,0:T(1,128)} custom-call(s32[1,128]{1,0:T(1,128)} %bitcast.2, bf16[128,4096]{1,0:T(8,128)(2,1)} %emb_hbm.1), custom_call_target="tpu_custom_call" | custom-call | tf_op jit(solution)/shard_map/pallas_call | solution.py:193
  56.6 0.0 copy-start
  56.6 0.6 %copy-done = f32[1,128]{1,0:T(1,128)S(1)} copy-done((f32[1,128]{1,0:T(1,128)S(1)}, f32[1,128]{1,0:T(1,128)}, u32[]{:S(2)}) %copy-start) | copy-done | bytes 536
  57.2 0.5 copy.4
Async XLA Ops:
  56.6 0.6 %copy-start = (f32[1,128]{1,0:T(1,128)S(1)}, f32[1,128]{1,0:T(1,128)}, u32[]{:S(2)}) copy-start(f32[1,128]{1,0:T(1,128)} %shard_map.28) | copy-start | bytes 1540

commit v3 on v2

--- a/solution.py
+++ b/solution.py
@@ -20,13 +20,22 @@
 EMPTY_SCORE = 2.0
 
 
+WHEN = (3, 2, 0, 1)
+
+
+def axes(o):
+    return sum(k != 0 for k in o[:3])
+
+
 def order():
     every = [(x, z, y, c) for x in range(4) for z in range(4) for y in range(4) for c in range(2)]
     random.Random(0).shuffle(every)
-    return sorted(every, key=lambda o: (-sum(min(k, 4 - k) for k in o[:3]), -o[3]))
+    distance = lambda o: sum(min(k, 4 - k) for k in o[:3])
+    return sorted(every, key=lambda o: (WHEN[axes(o)], -distance(o), -o[3]))
 
 
 ORDER = order()
+FIRST = 54
 
 
 def code(o):
@@ -65,7 +74,7 @@
 def kernel(
     ids_hbm, emb_hbm, out_ref,
     ids_ref, emb_ref, blocks, outgoing, incoming, members, index_v, index_s, highest, returned,
-    ids_sem, emb_sem, index_sem, send_sem, recv_sem, back_send_sem, back_recv_sem,
+    ids_sem, emb_sem, index_sem, send_sem, recv_sem, back_send_sem, back_recv_sem, entered,
 ):
     me = position()
     around = Around(me)
@@ -73,13 +82,11 @@
 
     ids_in = pltpu.make_async_copy(ids_hbm, ids_ref, ids_sem)
     ids_in.start()
-    rows_in = []
-    for g in range(ROWS // GROUP):
-        group = pl.ds(g * GROUP, GROUP)
-        rows_in.append(pltpu.make_async_copy(emb_hbm.at[group], emb_ref.at[group], emb_sem.at[g]))
-        rows_in[g].start()
-
-    for o in ORDER[:-1]:
+    rows_in = pltpu.make_async_copy(emb_hbm, emb_ref, emb_sem)
+    rows_in.start()
+
+    planes = [o for o in ORDER[:-1] if axes(o) < 3]
+    for o in planes:
         pl.semaphore_signal(barrier, inc=1, device_id=around.back(o), device_id_type=MESH)
 
     rows = lax.broadcasted_iota(jnp.int32, (ROWS, DEVICES), 0)
@@ -103,8 +110,8 @@
     swap = ((a // Q == b % GROUP) & (a % Q == b // GROUP)).astype(jnp.bfloat16)
 
     blocks[ROWS] = jnp.full((Q, W), EMPTY, jnp.bfloat16)
+    rows_in.wait()
     for g in range(ROWS // GROUP):
-        rows_in[g].wait()
         values = emb_ref[pl.ds(g * GROUP, GROUP)].astype(jnp.float32)
         squares = jnp.sum(values * values, axis=1, keepdims=True)
         normed = (values * lax.rsqrt(squares + 1e-06)).astype(jnp.bfloat16)
@@ -113,9 +120,13 @@
         blocks[pl.ds(g * GROUP, GROUP)] = swapped.reshape(GROUP, Q, W)
 
     to_scalars.wait()
-    pl.semaphore_wait(barrier, DEVICES - 1)
+    pl.semaphore_wait(barrier, len(planes))
+    for k in range(1, 4):
+        pl.semaphore_signal(entered, inc=1, device_id=around.to((k, 0, 0, 0)), device_id_type=MESH)
 
     for n, o in enumerate(ORDER[:-1]):
+        if n == FIRST:
+            pl.semaphore_wait(entered, 3)
         for p in range(CAP):
             outgoing[n, p] = blocks[index_s[p, code(o)]]
         pltpu.make_async_remote_copy(
@@ -207,17 +218,21 @@
             pltpu.VMEM((DEVICES, 1, 128), jnp.float32),
             pltpu.VMEM((DEVICES, 1, 128), jnp.float32),
             pltpu.SemaphoreType.DMA,
-            pltpu.SemaphoreType.DMA((ROWS // GROUP,)),
+            pltpu.SemaphoreType.DMA,
             pltpu.SemaphoreType.DMA,
             pltpu.SemaphoreType.DMA,
             pltpu.SemaphoreType.DMA((GROUPS,)),
             pltpu.SemaphoreType.DMA,
             pltpu.SemaphoreType.DMA,
+            pltpu.SemaphoreType.REGULAR,
         ],
         compiler_params=pltpu.CompilerParams(
-            collective_id=0, has_side_effects=True, vmem_limit_bytes=62 * 1024 * 1024
+            collective_id=0, has_side_effects=True, vmem_limit_bytes=40 * 1024 * 1024
         ),
-    )(cluster_ids.reshape(1, ROWS), embeddings)
+    )(
+        pltpu.with_memory_space_constraint(cluster_ids.reshape(1, ROWS), pltpu.HBM),
+        pltpu.with_memory_space_constraint(embeddings, pltpu.HBM),
+    )
     return out.reshape(ROWS)
 
 

time: 57.8 us -> 55.5 us (0.960)
  Pallas kernels: 56.6 us -> 54.9 us
  local copies, waits for them, and re-layouts: 1.1 us -> 0.51 us
    pallas_call x1, Pallas kernels: 56.6 us -> 54.9 us  [body(): pl.pallas_call(kernel, out_shape=jax.ShapeDtypeStruct((1, ROWS), jnp.floa...]
    unnamed x3 -> x1, local copies, waits for them, and re-layouts: 1.1 us -> 0.51 us
where the time goes in v3:
time: 55.5 us; the launch traced here: 55.4 us
  Pallas kernels  54.9 us (99%)
    pallas_call x1, Pallas kernels, body(): pl.pallas_call(kernel, out_shape=jax.ShapeDtypeStruct((1, ROWS), jnp.floa...  54.9 us

profile of v3, /device:TPU:1, one launch (start us, length us, event | category | flops | bytes accessed | tf_op | source)
XLA Modules:
  0.0 55.4 jit_solution(4015606351790352875)
XLA Ops:
  0.0 54.9 %shard_map.28 = f32[1,128]{1,0:T(1,128)S(1)} custom-call(s32[1,128]{1,0:T(1,128)} %bitcast.3, bf16[128,4096]{1,0:T(8,128)(2,1)} %emb_hbm.1), custom_call_target="tpu_custom_call" | custom-call | tf_op jit(solution)/shard_map/pallas_call | solution.py:204
  54.9 0.5 copy.4

commit v4 on v3

--- a/solution.py
+++ b/solution.py
@@ -27,10 +27,13 @@
     return sum(k != 0 for k in o[:3])
 
 
+def distance(o):
+    return sum(min(k, 4 - k) for k in o[:3])
+
+
 def order():
     every = [(x, z, y, c) for x in range(4) for z in range(4) for y in range(4) for c in range(2)]
     random.Random(0).shuffle(every)
-    distance = lambda o: sum(min(k, 4 - k) for k in o[:3])
     return sorted(every, key=lambda o: (WHEN[axes(o)], -distance(o), -o[3]))
 
 
@@ -157,24 +160,37 @@
 
     arrive(GROUPS - 1, GROUP - 1)
 
+    split = 2 * DEVICES
     places = CAP * DEVICES
     scores = lax.dot_general(
-        members[...], members[...], (((1,), (1,)), ((), ())), preferred_element_type=jnp.float32
-    )
-    i = lax.broadcasted_iota(jnp.int32, (places, places), 0)
-    j = lax.broadcasted_iota(jnp.int32, (places, places), 1)
-    own = jnp.sum(jnp.where(i == j, scores, 0.0), axis=0, keepdims=True)
-    allowed = (own < EMPTY_SCORE) & (i != j)
-    best = jnp.max(jnp.where(allowed, scores, -1.0), axis=1, keepdims=True)
+        members[...], members[:split], (((1,), (1,)), ((), ())), preferred_element_type=jnp.float32
+    )
+    corner = lax.dot_general(
+        members[split:], members[split:], (((1,), (1,)), ((), ())), preferred_element_type=jnp.float32
+    )
+    i = lax.broadcasted_iota(jnp.int32, (places, split), 0)
+    j = lax.broadcasted_iota(jnp.int32, (places, split), 1)
+    first = jnp.sum(jnp.where(i == j, scores, 0.0), axis=0, keepdims=True) < EMPTY_SCORE
+    own = jnp.where(rows == lanes, corner, 0.0)
+    last = jnp.sum(own, axis=0, keepdims=True) < EMPTY_SCORE
+    last_rows = jnp.sum(own, axis=1, keepdims=True) < EMPTY_SCORE
+    best = jnp.max(jnp.where(first & (i != j), scores, -1.0), axis=1, keepdims=True)
+    across = jnp.max(jnp.where(last_rows, scores[split:], -1.0), axis=0, keepdims=True)
+    turned = [
+        jnp.max(jnp.where(rows == lanes, across[:, k * DEVICES : (k + 1) * DEVICES], -1.0), axis=1, keepdims=True)
+        for k in range(2)
+    ]
+    inside = jnp.max(jnp.where(last & (rows != lanes), corner, -1.0), axis=1, keepdims=True)
+    best = jnp.maximum(best, jnp.concatenate([*turned, inside], axis=0))
     by_place = jnp.where(
         lanes == 0, best[:DEVICES], jnp.where(lanes == 1, best[DEVICES : 2 * DEVICES], best[2 * DEVICES :])
     )
     highest[...] = by_place.reshape(DEVICES, 1, 128)
     returned[0] = by_place[DEVICES - 1 :]
 
-    for n, o in enumerate(ORDER[:-1]):
+    for o in sorted(ORDER[:-1], key=distance, reverse=True):
         pltpu.make_async_remote_copy(
-            src_ref=highest.at[n],
+            src_ref=highest.at[ORDER.index(o)],
             dst_ref=returned.at[code(o)],
             send_sem=back_send_sem,
             recv_sem=back_recv_sem,

time: 55.5 us -> 55 us (level)
  Pallas kernels: 54.9 us -> 54.3 us
where the time goes in v4:
time: 55 us; the launch traced here: 54.8 us
  Pallas kernels  54.3 us (99%)
    pallas_call x1, Pallas kernels, body(): pl.pallas_call(kernel, out_shape=jax.ShapeDtypeStruct((1, ROWS), jnp.floa...  54.3 us

profile of v4, /device:TPU:1, one launch (start us, length us, event | category | flops | bytes accessed | tf_op | source)
XLA Modules:
  0.0 54.8 jit_solution(669606910119854034)
XLA Ops:
  0.0 54.3 %shard_map.28 = f32[1,128]{1,0:T(1,128)S(1)} custom-call(s32[1,128]{1,0:T(1,128)} %bitcast.3, bf16[128,4096]{1,0:T(8,128)(2,1)} %emb_hbm.1), custom_call_target="tpu_custom_call" | custom-call | tf_op jit(solution)/shard_map/pallas_call | solution.py:220
  54.3 0.5 copy.4

commit v5 on v4

--- a/solution.py
+++ b/solution.py
@@ -20,25 +20,27 @@
 EMPTY_SCORE = 2.0
 
 
-WHEN = (3, 2, 0, 1)
-
-
 def axes(o):
     return sum(k != 0 for k in o[:3])
 
 
 def distance(o):
     return sum(min(k, 4 - k) for k in o[:3])
+
+
+def turn(o):
+    return (4, 0, 1 if distance(o) > 2 else 3, 2)[axes(o)]
 
 
 def order():
     every = [(x, z, y, c) for x in range(4) for z in range(4) for y in range(4) for c in range(2)]
     random.Random(0).shuffle(every)
-    return sorted(every, key=lambda o: (WHEN[axes(o)], -distance(o), -o[3]))
+    return sorted(every, key=lambda o: (turn(o), -o[3], -distance(o)))
 
 
 ORDER = order()
-FIRST = 54
+TWO = [turn(o) for o in ORDER].index(1)
+THREE = [turn(o) for o in ORDER].index(2)
 
 
 def code(o):
@@ -77,7 +79,7 @@
 def kernel(
     ids_hbm, emb_hbm, out_ref,
     ids_ref, emb_ref, blocks, outgoing, incoming, members, index_v, index_s, highest, returned,
-    ids_sem, emb_sem, index_sem, send_sem, recv_sem, back_send_sem, back_recv_sem, entered,
+    ids_sem, emb_sem, index_sem, send_sem, recv_sem, back_send_sem, back_recv_sem, lines_known, planes_known,
 ):
     me = position()
     around = Around(me)
@@ -88,8 +90,8 @@
     rows_in = pltpu.make_async_copy(emb_hbm, emb_ref, emb_sem)
     rows_in.start()
 
-    planes = [o for o in ORDER[:-1] if axes(o) < 3]
-    for o in planes:
+    lines = [o for o in ORDER[:-1] if axes(o) < 2]
+    for o in lines:
         pl.semaphore_signal(barrier, inc=1, device_id=around.back(o), device_id_type=MESH)
 
     rows = lax.broadcasted_iota(jnp.int32, (ROWS, DEVICES), 0)
@@ -123,13 +125,17 @@
         blocks[pl.ds(g * GROUP, GROUP)] = swapped.reshape(GROUP, Q, W)
 
     to_scalars.wait()
-    pl.semaphore_wait(barrier, len(planes))
+    pl.semaphore_wait(barrier, len(lines))
     for k in range(1, 4):
-        pl.semaphore_signal(entered, inc=1, device_id=around.to((k, 0, 0, 0)), device_id_type=MESH)
-
+        for peer in ((k, 0, 0, 0), (0, 0, k, 0)):
+            pl.semaphore_signal(lines_known, inc=1, device_id=around.to(peer), device_id_type=MESH)
     for n, o in enumerate(ORDER[:-1]):
-        if n == FIRST:
-            pl.semaphore_wait(entered, 3)
+        if n == TWO:
+            pl.semaphore_wait(lines_known, 6)
+            for k in range(1, 4):
+                pl.semaphore_signal(planes_known, inc=1, device_id=around.to((k, 0, 0, 0)), device_id_type=MESH)
+        if n == THREE:
+            pl.semaphore_wait(planes_known, 3)
         for p in range(CAP):
             outgoing[n, p] = blocks[index_s[p, code(o)]]
         pltpu.make_async_remote_copy(
@@ -241,6 +247,7 @@
             pltpu.SemaphoreType.DMA,
             pltpu.SemaphoreType.DMA,
             pltpu.SemaphoreType.REGULAR,
+            pltpu.SemaphoreType.REGULAR,
         ],
         compiler_params=pltpu.CompilerParams(
             collective_id=0, has_side_effects=True, vmem_limit_bytes=40 * 1024 * 1024

time: 55 us -> 54 us (0.982)
  Pallas kernels: 54.3 us -> 53.4 us
    pallas_call x1, Pallas kernels: 54.3 us -> 53.4 us  [body(): pl.pallas_call(kernel, out_shape=jax.ShapeDtypeStruct((1, ROWS), jnp.floa...]
where the time goes in v5:
time: 54 us; the launch traced here: 53.9 us
  Pallas kernels  53.4 us (99%)
    pallas_call x1, Pallas kernels, body(): pl.pallas_call(kernel, out_shape=jax.ShapeDtypeStruct((1, ROWS), jnp.floa...  53.4 us

profile of v5, /device:TPU:1, one launch (start us, length us, event | category | flops | bytes accessed | tf_op | source)
XLA Modules:
  0.0 53.9 jit_solution(7064105383290269244)
XLA Ops:
  0.0 53.4 %shard_map.28 = f32[1,128]{1,0:T(1,128)S(1)} custom-call(s32[1,128]{1,0:T(1,128)} %bitcast.3, bf16[128,4096]{1,0:T(8,128)(2,1)} %emb_hbm.1), custom_call_target="tpu_custom_call" | custom-call | tf_op jit(solution)/shard_map/pallas_call | solution.py:226
  53.4 0.5 copy.4

commit v6 on v5

--- a/solution.py
+++ b/solution.py
@@ -35,7 +35,20 @@
 def order():
     every = [(x, z, y, c) for x in range(4) for z in range(4) for y in range(4) for c in range(2)]
     random.Random(0).shuffle(every)
-    return sorted(every, key=lambda o: (turn(o), -o[3], -distance(o)))
+    left = sorted(every, key=lambda o: (turn(o), -o[3], -distance(o)))
+    done = []
+    while left:
+        now = [o for o in left if turn(o) == turn(left[0])]
+
+        def clash(o):
+            return sum(
+                w * sum(a == b and a != 0 for a, b in zip(o[:3], q[:3])) for w, q in zip((8, 4, 2, 1), reversed(done))
+            )
+
+        best = min(now, key=clash)
+        left.remove(best)
+        done.append(best)
+    return done[:-2] + [(0, 0, 0, 1), (0, 0, 0, 0)]
 
 
 ORDER = order()
@@ -207,12 +220,13 @@
     back = returned.at[pl.ds(1, DEVICES - 1)]
     pltpu.make_async_copy(back, back, back_recv_sem).wait()
 
-    mine = jnp.dot(
-        named.astype(jnp.float32),
-        returned[...].reshape(DEVICES, 128),
-        precision=lax.Precision.HIGHEST,
-        preferred_element_type=jnp.float32,
-    )
+    picks = named.astype(jnp.bfloat16)
+    left = returned[...].reshape(DEVICES, 128)
+    mine = jnp.zeros((ROWS, 128), jnp.float32)
+    for _ in range(3):
+        part = left.astype(jnp.bfloat16)
+        mine += jnp.dot(picks, part, preferred_element_type=jnp.float32)
+        left = left - part.astype(jnp.float32)
     column = jnp.sum(jnp.where(lanes == place.astype(jnp.int32), mine, 0.0), axis=1, keepdims=True)
     out_ref[...] = jnp.sum(jnp.where(rows == lanes, column, 0.0), axis=0, keepdims=True)
 

time: 54 us -> 53.6 us (level)
  no operation moved by 1% of the time
where the time goes in v6:
time: 53.6 us; the launch traced here: 53.5 us
  Pallas kernels  53 us (99%)
    pallas_call x1, Pallas kernels, body(): pl.pallas_call(kernel, out_shape=jax.ShapeDtypeStruct((1, ROWS), jnp.floa...  53 us

profile of v6, /device:TPU:1, one launch (start us, length us, event | category | flops | bytes accessed | tf_op | source)
XLA Modules:
  0.0 53.5 jit_solution(6179127961750696915)
XLA Ops:
  0.0 53.0 %shard_map.28 = f32[1,128]{1,0:T(1,128)S(1)} custom-call(s32[1,128]{1,0:T(1,128)} %bitcast.3, bf16[128,4096]{1,0:T(8,128)(2,1)} %emb_hbm.1), custom_call_target="tpu_custom_call" | custom-call | tf_op jit(solution)/shard_map/pallas_call | solution.py:240
  53.0 0.5 copy.4

commit v7 on v6

--- a/solution.py
+++ b/solution.py
@@ -151,14 +151,15 @@
             pl.semaphore_wait(planes_known, 3)
         for p in range(CAP):
             outgoing[n, p] = blocks[index_s[p, code(o)]]
-        pltpu.make_async_remote_copy(
-            src_ref=outgoing.at[n],
-            dst_ref=incoming.at[n],
-            send_sem=send_sem,
-            recv_sem=recv_sem.at[n // GROUP],
-            device_id=around.to(o),
-            device_id_type=MESH,
-        ).start()
+        for part in (pl.ds(0, 2), pl.ds(2, 1)):
+            pltpu.make_async_remote_copy(
+                src_ref=outgoing.at[n, part],
+                dst_ref=incoming.at[n, part],
+                send_sem=send_sem,
+                recv_sem=recv_sem.at[n // GROUP],
+                device_id=around.to(o),
+                device_id_type=MESH,
+            ).start()
 
     for p in range(CAP):
         incoming[DEVICES - 1, p] = blocks[index_s[p, 0]]

time: 53.6 us -> 53.6 us (level)
  no operation moved by 1% of the time
where the time goes in v7:
time: 53.6 us; the launch traced here: 53.5 us
  Pallas kernels  53 us (99%)
    pallas_call x1, Pallas kernels, body(): pl.pallas_call(kernel, out_shape=jax.ShapeDtypeStruct((1, ROWS), jnp.floa...  53 us

profile of v7, /device:TPU:1, one launch (start us, length us, event | category | flops | bytes accessed | tf_op | source)
XLA Modules:
  0.0 53.5 jit_solution(11492550687098400195)
XLA Ops:
  0.0 53.0 %shard_map.28 = f32[1,128]{1,0:T(1,128)S(1)} custom-call(s32[1,128]{1,0:T(1,128)} %bitcast.3, bf16[128,4096]{1,0:T(8,128)(2,1)} %emb_hbm.1), custom_call_target="tpu_custom_call" | custom-call | tf_op jit(solution)/shard_map/pallas_call | solution.py:241
  53.0 0.5 copy.4
